TPU v7x, 512 devices: a whole 4x8x8 slice. The times are simulated.
512 devices in a mesh: ka: 64 (over z, x, y_lo), ta: 8 (over y_hi, core).
Axes of the slice: x: 4, y: 8 (y_hi: 4, y_lo: 2; y = y_hi * 2 + y_lo), z: 8, core: 2. Of those that a mesh axis runs over, the one named last changes fastest.
Arguments:
- green_time: bfloat16 [2048, 256, 256], P(('ta', 'ka')), parts along dimension 0, may hold values from -0.375 to 0.375
- orbitals: bfloat16 [256, 256, 512], P('ka'), may hold values from -3.296875 to 3.296875
- pair_table: int32 [256, 256], P(None, 'ka'), may hold values from 0 to 255, as said below
- pair_momenta: int32 [2], replicated, may hold values from 0 to 255
- owner_rows: int32 [512], replicated, may hold values from 0 to 511, each once
Outputs:
- bubble: float32 [4096, 2, 512], P(('ta', 'ka')), parts along dimension 0
There are 8 independent parts, one for each index of `ta`. A program takes and returns all parts, laid end to end along the dimension named above; an argument that names none is the same for every part. Nothing has to cross between parts.
Inputs may be any that keep to these rules, and one draw needn't show every extreme that they name: The momenta form a 4 x 4 x (16) periodic lattice listed in an order drawn from the seed; row a of pair_table gives, for each k, the index of momentum a minus momentum k, so every row is a permutation of 0 to 255.
All inputs are finite; a program needn't handle non-finite values.
Results may differ from a plain program's by a relative error of at most 0.0057.
Values may be sent and summed in bfloat16 or wider, within the bound.
A program may use at most 64 MiB of HBM per device.

v0:
```python
import jax
import jax.numpy as jnp
from jax import lax
from jax.sharding import PartitionSpec as P


def per_device(green_time, orbitals, pair_table, pair_momenta, owner_rows):
    orbitals_owned = jnp.take(orbitals, owner_rows, axis=2)
    half_product = jnp.einsum(
        "kij,kjp->kip", green_time, orbitals, preferred_element_type=jnp.float32
    ).astype(jnp.bfloat16)
    projected = jnp.einsum(
        "kia,kip->kap", orbitals_owned, half_product, preferred_element_type=jnp.float32
    ).astype(jnp.bfloat16)
    local_pairs = jnp.take(pair_table, pair_momenta, axis=0)
    partners = lax.all_gather(local_pairs, "ka", axis=1, tiled=True)
    inverse_count = 1.0 / partners.shape[1]
    spread = lax.all_to_all(projected, "ka", split_axis=1, concat_axis=0, tiled=True)
    partner_blocks = jnp.take(spread, partners, axis=0)
    returned = lax.all_to_all(partner_blocks, "ka", split_axis=1, concat_axis=2, tiled=True)
    return lax.psum_scatter(
        jnp.einsum("kac,qkac->aqc", projected, returned, preferred_element_type=jnp.float32)
        * inverse_count,
        "ka",
        scatter_dimension=0,
        tiled=True,
    )


def solution(mesh):
    return jax.shard_map(
        per_device,
        mesh=mesh,
        in_specs=(P(("ta", "ka"), None, None), P("ka", None, None), P(None, "ka"), P(), P()),
        out_specs=P(("ta", "ka"), None, None),
        check_vma=False,
    )
```

profile of v0, /device:TPU:16, one launch (start us, length us, event | category | flops | bytes accessed | tf_op | source)
XLA Modules:
  0.0 922.7 jit_solution(13758151225031022009)
XLA Ops:
  6.5 0.7 compare_select_fusion.1
  7.3 0.7 compare_and_fusion.1
  8.0 1.7 copy.32
  9.7 2.4 gather_fusion.1
  12.1 2.7 select_bitcast_fusion
  14.7 4.5 bitcast_convert_fusion
  19.2 2.9 copy.34
  22.1 14.8 %all-to-all-start = ((bf16[4,512,512]{2,0,1:T(4,128)(2,1)}), bf16[4,512,512]{2,0,1:T(4,128)(2,1)S(1)}, u32[]{:S(2)}, u32[]{:S(2)}) async-start(bf16[4,512,512]{2,0,1:T(4,128)(2,1)} %copy.34), calls=%async_computation | async-start | bytes 4194304 | tf_op jit(solution)/shard_map/all_to_all | solution.py:18
  37.0 0.1 copy.29
  37.2 0.6 gather_fusion
  37.8 173.9 %all-gather = s32[64,4,2]{1,2,0:T(2,128)S(1)} all-gather(s32[1,4,2]{1,2,0:T(2,128)S(1)} %select_bitcast_fusion.1), channel_id=1, replica_groups=mesh['ka'=64,'ta'=8] {'ka'}, dimensions={0}, use_global_device_ids=true | all-gather | bytes 2080 | tf_op jit(solution)/shard_map/all_gather | solution.py:16
  211.7 0.1 reshape.44
  211.9 0.2 copy.31
  212.1 0.4 copy.61
  212.5 0.3 copy.36
  212.8 3.5 gather_fusion.2
  216.3 2.6 copy_select_fusion
  218.9 73.9 %all_to_all.36 = bf16[2,256,8,512]{3,2,0,1:T(8,128)(2,1)S(1)} all-to-all(bf16[2,256,8,512]{3,2,0,1:T(8,128)(2,1)S(1)} %copy_select_fusion), channel_id=1, replica_groups=mesh['ka'=64,'ta'=8] {'ka'}, dimensions={1} | all-to-all | bytes 8388608 | tf_op jit(solution)/shard_map/all_to_all | solution.py:20
  292.7 1.2 multiply_reduce_fusion
  293.9 0.2 broadcast_multiply_fusion
  294.1 2.9 copy.60
  297.1 1.3 dynamic-slice
  299.0 615.5 %all-reduce.3.cloned.1.call-done = f32[512,2,512]{2,1,0:T(2,128)} async-done(((f32[512,2,512]{2,1,0:T(2,128)}), f32[512,2,512]{2,1,0:T(2,128)}) %all-reduce.3.cloned.1.call-update) | async-done | bytes 2097168
  914.5 1.4 constant_dynamic-slice_fusion
  (21 shorter events, 0.2 us)
Async XLA Ops:
  6.5 8.2 copy-start
  19.2 17.8 %copy-start.2 = (s32[256,4]{0,1:T(4,128)S(1)}, s32[256,4]{0,1:T(4,128)}, u32[]{:S(2)}) copy-start(s32[256,4]{0,1:T(4,128)} %param.7) | copy-start | bytes 12292
  19.2 18.0 %copy-start.3 = (s32[2]{0:T(128)S(1)}, s32[2]{0:T(128)}, u32[]{:S(2)}) copy-start(s32[2]{0:T(128)} %param.8) | copy-start | bytes 28
  22.1 189.9 %all-to-all-start = ((bf16[4,512,512]{2,0,1:T(4,128)(2,1)}), bf16[4,512,512]{2,0,1:T(4,128)(2,1)S(1)}, u32[]{:S(2)}, u32[]{:S(2)}) async-start(bf16[4,512,512]{2,0,1:T(4,128)(2,1)} %copy.34), calls=%async_computation | async-start | bytes 4194304 | tf_op jit(solution)/shard_map/all_to_all | solution.py:18
  36.9 877.5 %all-reduce.3.cloned.1.call-start = ((), (), s32[]{:S(2)}) async-start(), calls=%async_computation.2 | async-start | bytes 4194304
  218.9 73.9 %copy-start.1 = (f32[512,512,4]{1,0,2:T(8,128)S(1)}, f32[512,512,4]{1,0,2:T(8,128)}, u32[]{:S(2)}) copy-start(f32[512,512,4]{1,0,2:T(8,128)} %get-tuple-element.5) | copy-start | bytes 12582916
Sparse Core Ops, SparseCore 0:
  297.2 617.2 all-reduce.2
where the time goes:
time: 923 us
  waiting for transfers between devices  615 us (67%)
  blocking collectives  248 us (27%)
  local copies, waits for them, and re-layouts  17.7 us (2%)
  starting transfers between devices  14.8 us (2%)
  between operations  14.2 us (2%)
    unnamed x2, waiting for transfers between devices  615 us
    all_gather x1, blocking collectives, per_device(): partners = lax.all_gather(local_pairs, 'ka', axis=1, tiled=True)  174 us
    all_to_all x1, blocking collectives, per_device(): lax.all_to_all(partner_blocks, 'ka', split_axis=1, concat_axis=2, tiled=T...  73.9 us
  transfers between devices with their start and end apart: 2, of which 1 were waited for; matrix products, arithmetic and copies ran while one was open for 0% of the time, Pallas kernels for 0%

commit v1 on v0

--- a/solution.py
+++ b/solution.py
@@ -13,7 +13,9 @@
         "kia,kip->kap", orbitals_owned, half_product, preferred_element_type=jnp.float32
     ).astype(jnp.bfloat16)
     local_pairs = jnp.take(pair_table, pair_momenta, axis=0)
-    partners = lax.all_gather(local_pairs, "ka", axis=1, tiled=True)
+    partners = jnp.concatenate(
+        lax.all_to_all(jnp.stack([local_pairs] * lax.axis_size("ka")), "ka", 0, 0), axis=1
+    )
     inverse_count = 1.0 / partners.shape[1]
     spread = lax.all_to_all(projected, "ka", split_axis=1, concat_axis=0, tiled=True)
     partner_blocks = jnp.take(spread, partners, axis=0)

time: 923 us -> 843 us (0.913)
  blocking collectives: 248 us -> 103 us
  waiting for transfers between devices: 615 us -> 665 us
  starting transfers between devices: 14.8 us -> 26 us
    all_gather x1 -> x0, blocking collectives: 174 us -> none  [per_device(): partners = lax.all_gather(local_pairs, 'ka', axis=1, tiled=True)]
    all_to_all x1, waiting for transfers between devices: 0.01 us -> 49.4 us  [per_device(): lax.all_to_all(projected, 'ka', split_axis=1, concat_axis=0, tiled=True)]
    all_to_all x1, blocking collectives: 73.9 us -> 103 us  [per_device(): lax.all_to_all(partner_blocks, 'ka', split_axis=1, concat_axis=2, tiled=T...]
    all_to_all x0 -> x1, starting transfers between devices: none -> 14.8 us  [per_device(): lax.all_to_all(jnp.stack([local_pairs] * lax.axis_size('ka')), 'ka', 0, 0)]
  transfers between devices with their start and end apart: 2 -> 3, of which waited for: 1 -> 2; matrix products, arithmetic and copies ran while one was open for 0% -> 2% of each run, Pallas kernels for 0% -> 0%
where the time goes in v1:
time: 843 us; the launch traced here: 842 us
  waiting for transfers between devices  665 us (79%)
  blocking collectives  103 us (12%)
  starting transfers between devices  26 us (3%)
  local copies, waits for them, and re-layouts  19.2 us (2%)
  between operations  14.2 us (2%)
  other arithmetic  9.49 us (1%)
    unnamed x2, waiting for transfers between devices  616 us
    all_to_all x1, blocking collectives, per_device(): lax.all_to_all(partner_blocks, 'ka', split_axis=1, concat_axis=2, tiled=T...  103 us
    all_to_all x1, waiting for transfers between devices, per_device(): lax.all_to_all(projected, 'ka', split_axis=1, concat_axis=0, tiled=True)  49.4 us
  transfers between devices with their start and end apart: 3, of which 2 were waited for; matrix products, arithmetic and copies ran while one was open for 2% of the time, Pallas kernels for 0%

profile of v1, /device:TPU:16, one launch (start us, length us, event | category | flops | bytes accessed | tf_op | source)
XLA Modules:
  0.0 842.1 jit_solution(17705653232876483384)
XLA Ops:
  6.5 0.7 compare_select_fusion.3
  7.3 0.7 compare_and_fusion.2
  7.9 0.8 copy.27
  8.7 0.6 gather_fusion
  9.4 0.7 stack.2
  10.0 14.8 %all-to-all-start = ((s32[64,2,4]{2,1,0:T(2,128)}), s32[64,2,4]{2,1,0:T(2,128)S(1)}, u32[]{:S(2)}, u32[]{:S(2)}) async-start(s32[64,2,4]{2,1,0:T(2,128)} %stack.2), calls=%async_computation | async-start | bytes 131072 | tf_op jit(solution)/shard_map/all_to_all | solution.py:17
  24.8 0.7 compare_select_fusion.2
  25.5 0.7 compare_and_fusion.1
  26.2 1.7 copy.30
  27.9 2.4 gather_fusion.1
  30.3 2.7 select_bitcast_fusion
  33.0 4.5 bitcast_convert_fusion
  37.4 2.9 copy.32
  40.4 11.2 %all-to-all-start.1 = ((bf16[4,512,512]{2,0,1:T(4,128)(2,1)}), bf16[4,512,512]{2,0,1:T(4,128)(2,1)S(1)}, u32[]{:S(2)}, u32[]{:S(2)}) async-start(bf16[4,512,512]{2,0,1:T(4,128)(2,1)} %copy.32), calls=%async_computation.1 | async-start | bytes 4194304 | tf_op jit(solution)/shard_map/all_to_all | solution.py:20
  52.1 49.4 %all-to-all-done.1 = bf16[4,512,512]{2,0,1:T(4,128)(2,1)S(1)} async-done(((bf16[4,512,512]{2,0,1:T(4,128)(2,1)}), bf16[4,512,512]{2,0,1:T(4,128)(2,1)S(1)}, u32[]{:S(2)}, u32[]{:S(2)}) %all-to-all-start.1) | async-done | bytes 2097184 | tf_op jit(solution)/shard_map/all_to_all | solution.py:20
  101.5 0.4 copy.60
  102.2 3.5 gather_fusion.2
  105.7 2.6 copy_select_fusion
  108.3 103.4 %all_to_all.41 = bf16[2,256,8,512]{3,2,0,1:T(8,128)(2,1)S(1)} all-to-all(bf16[2,256,8,512]{3,2,0,1:T(8,128)(2,1)S(1)} %copy_select_fusion), channel_id=1, replica_groups=mesh['ka'=64,'ta'=8] {'ka'}, dimensions={1} | all-to-all | bytes 8388608 | tf_op jit(solution)/shard_map/all_to_all | solution.py:22
  211.7 1.2 multiply_reduce_fusion
  213.1 2.9 copy.59
  216.1 1.3 dynamic-slice
  218.0 615.9 %all-reduce.3.cloned.1.call-done = f32[512,2,512]{2,1,0:T(2,128)} async-done(((f32[512,2,512]{2,1,0:T(2,128)}), f32[512,2,512]{2,1,0:T(2,128)}) %all-reduce.3.cloned.1.call-update) | async-done | bytes 2097168
  833.9 1.4 constant_dynamic-slice_fusion
  (20 shorter events, 1.1 us)
Async XLA Ops:
  6.5 26.4 %copy-start = (bf16[4,256,256]{2,1,0:T(8,128)(2,1)S(1)}, bf16[4,256,256]{2,1,0:T(8,128)(2,1)}, u32[]{:S(2)}) copy-start(bf16[4,256,256]{2,1,0:T(8,128)(2,1)} %param.5) | copy-start | bytes 1572868
  10.0 30.3 %all-to-all-start = ((s32[64,2,4]{2,1,0:T(2,128)}), s32[64,2,4]{2,1,0:T(2,128)S(1)}, u32[]{:S(2)}, u32[]{:S(2)}) async-start(s32[64,2,4]{2,1,0:T(2,128)} %stack.2), calls=%async_computation | async-start | bytes 131072 | tf_op jit(solution)/shard_map/all_to_all | solution.py:17
  40.4 61.1 %all-to-all-start.1 = ((bf16[4,512,512]{2,0,1:T(4,128)(2,1)}), bf16[4,512,512]{2,0,1:T(4,128)(2,1)S(1)}, u32[]{:S(2)}, u32[]{:S(2)}) async-start(bf16[4,512,512]{2,0,1:T(4,128)(2,1)} %copy.32), calls=%async_computation.1 | async-start | bytes 4194304 | tf_op jit(solution)/shard_map/all_to_all | solution.py:20
  51.6 782.3 %all-reduce.3.cloned.1.call-start = ((), (), s32[]{:S(2)}) async-start(), calls=%async_computation.3 | async-start | bytes 4194304
  108.3 103.4 %copy-start.1 = (f32[512,512,4]{1,0,2:T(8,128)S(1)}, f32[512,512,4]{1,0,2:T(8,128)}, u32[]{:S(2)}) copy-start(f32[512,512,4]{1,0,2:T(8,128)} %get-tuple-element.5) | copy-start | bytes 12582916
Sparse Core Ops, SparseCore 0:
  216.2 617.6 all-reduce.2
